TPU v7x, 32 devices: a whole 2x2x4 slice. The times are simulated.
32 devices in a mesh: grp: 2 (over y), blk: 8 (over z, core), tm: 2 (over x), rep: 1.
Axes of the slice: x: 2, y: 2, z: 4, core: 2. Of those that a mesh axis runs over, the one named last changes fastest.
Arguments:
- factor_rows: bfloat16 [8192, 2048], P(('grp', 'blk')), parts along dimension 0, may hold values from -0.125 to 0.125
- noise: bfloat16 [8192, 8192], P(('grp', 'blk'), ('tm', 'rep')), parts along dimension 0, may hold values from -6 to 6
- time_kernel: float32 [8192], replicated, may hold values from -0.0625 to 0.0625
- region_of_block: int32 [16], P('grp'), parts along dimension 0, may hold values from 0 to 3, as said below
Outputs:
- field: bfloat16 [8192, 8192], P(('grp', 'blk', 'tm', 'rep')), parts along dimension 0
There are 2 independent parts, one for each index of `grp`. A program takes and returns all parts, laid end to end along the dimension named above; an argument that names none is the same for every part. Nothing has to cross between parts.
Inputs may be any that keep to these rules, and one draw needn't show every extreme that they name: `region_of_block`: each part is its own table: within one part, the blocks of one region are consecutive, region numbers never fall from block to block and every region from 0 to 3 appears; a region holds 1 to 4 blocks, and some region holds exactly 4. The next part starts again at region 0.
All inputs are finite; a program needn't handle non-finite values.
Results may differ from a plain program's by a relative error of at most 0.0049.
Values may be sent and summed in bfloat16 or wider, within the bound.
A program may use at most 128 MiB of HBM per device.

v0:
```python
import math

import jax
import jax.numpy as jnp
from jax import lax
from jax.sharding import PartitionSpec as P

FIRST = 64


def shifted(block, axis, distance):
    devices = range(lax.axis_size(axis))
    route = [(i - distance, i) for i in devices if i - distance in devices]
    return lax.ppermute(block, axis, route)


def make_tables(first, second):
    total = first * second
    row_a = lax.broadcasted_iota(jnp.int32, (first, first), 0)
    col_a = lax.broadcasted_iota(jnp.int32, (first, first), 1)
    angle_one = 2.0 * math.pi / first * (row_a * col_a % first).astype(jnp.float32)
    row_t = lax.broadcasted_iota(jnp.int32, (first, second), 0)
    col_t = lax.broadcasted_iota(jnp.int32, (first, second), 1)
    angle_tw = 2.0 * math.pi / total * (row_t * col_t % total).astype(jnp.float32)
    row_b = lax.broadcasted_iota(jnp.int32, (second, second), 0)
    col_b = lax.broadcasted_iota(jnp.int32, (second, second), 1)
    angle_two = 2.0 * math.pi / second * (row_b * col_b % second).astype(jnp.float32)
    return (
        jnp.cos(angle_one),
        -jnp.sin(angle_one),
        jnp.cos(angle_tw),
        -jnp.sin(angle_tw),
        jnp.cos(angle_two),
        -jnp.sin(angle_two),
    )


def left_apply(table, values):
    return jnp.einsum(
        "kn,rnm->rkm", table, values.astype(jnp.float32), precision=lax.Precision.HIGH
    )


def right_apply(values, table):
    return jnp.einsum("rkn,nm->rkm", values, table, precision=lax.Precision.HIGH)


def forward(sig_re, sig_im, tables):
    one_re, one_im, tw_re, tw_im, two_re, two_im = tables
    first_re = left_apply(one_re, sig_re) - left_apply(one_im, sig_im)
    first_im = left_apply(one_re, sig_im) + left_apply(one_im, sig_re)
    turned_re = first_re * tw_re - first_im * tw_im
    turned_im = first_re * tw_im + first_im * tw_re
    spec_re = right_apply(turned_re, two_re) - right_apply(turned_im, two_im)
    spec_im = right_apply(turned_re, two_im) + right_apply(turned_im, two_re)
    return (spec_re, spec_im)


def inverse(spec_re, spec_im, tables):
    one_re, one_im, tw_re, tw_im, two_re, two_im = tables
    back_re = right_apply(spec_re, two_re) + right_apply(spec_im, two_im)
    back_im = right_apply(spec_im, two_re) - right_apply(spec_re, two_im)
    turned_re = back_re * tw_re + back_im * tw_im
    turned_im = back_im * tw_re - back_re * tw_im
    total = one_re.shape[0] * two_re.shape[0]
    out_re = (left_apply(one_re, turned_re) + left_apply(one_im, turned_im)) / total
    out_im = (left_apply(one_re, turned_im) - left_apply(one_im, turned_re)) / total
    return (out_re, out_im)


def on_device(factor_rows, noise, time_kernel, region_of_block):
    width = noise.shape[0]
    slots = factor_rows.shape[1] // width
    position = lax.axis_index("blk")
    own_region = lax.dynamic_index_in_dim(region_of_block, position, 0, keepdims=False)
    row_ids = lax.broadcasted_iota(jnp.int32, (width, width), 0)
    col_ids = lax.broadcasted_iota(jnp.int32, (width, width), 1)
    diagonal_tile = jnp.where(
        row_ids >= col_ids, factor_rows[:, :width], jnp.zeros((width, width), jnp.bfloat16)
    )
    total = jnp.dot(diagonal_tile, noise, preferred_element_type=jnp.float32)
    previous = noise
    for step in range(1, slots):
        previous = shifted(noise, "blk", step)
        source = jnp.maximum(position - step, 0)
        source_region = lax.dynamic_index_in_dim(region_of_block, source, 0, keepdims=False)
        valid = (position >= step) & (source_region == own_region)
        tile = factor_rows[:, step * width : (step + 1) * width]
        product = jnp.dot(tile, previous, preferred_element_type=jnp.float32)
        total = total + jnp.where(valid, product, jnp.zeros_like(product))
    spatial = total.astype(jnp.bfloat16)
    regrouped = lax.all_to_all(spatial, ("tm", "rep"), split_axis=0, concat_axis=1, tiled=True)
    days = regrouped.shape[1]
    stations = regrouped.shape[0]
    second = days // FIRST
    tables = make_tables(FIRST, second)
    paired = regrouped.reshape(stations // 2, 2, FIRST, second)
    sig_re = paired[:, 0]
    sig_im = paired[:, 1]
    kernel_sig = time_kernel.reshape(1, FIRST, second)
    kernel_re, kernel_im = forward(kernel_sig, jnp.zeros_like(kernel_sig), tables)
    spec_re, spec_im = forward(sig_re, sig_im, tables)
    prod_re = spec_re * kernel_re - spec_im * kernel_im
    prod_im = spec_re * kernel_im + spec_im * kernel_re
    out_re, out_im = inverse(prod_re, prod_im, tables)
    joined = jnp.stack((out_re, out_im), axis=1)
    return joined.reshape(stations, days).astype(jnp.bfloat16)


def solution(mesh):
    placed = (P(("grp", "blk"), None), P(("grp", "blk"), ("tm", "rep")), P(), P("grp"))
    return jax.shard_map(
        on_device,
        mesh=mesh,
        in_specs=placed,
        out_specs=P(("grp", "blk", "tm", "rep"), None),
        check_vma=False,
    )
```

profile of v0, /device:TPU:24, one launch (start us, length us, event | category | flops | bytes accessed | tf_op | source)
XLA Modules:
  0.0 406.4 jit_solution(16711541420971721130)
XLA Ops:
  0.0 1.4 collective-permute-start.1
  1.4 1.9 collective-permute-start
  4.7 1.4 fusion.214
  9.8 4.8 %fusion.41 = f32[512,4096]{1,0:T(8,128)S(1)} fusion(bf16[512,4096]{1,0:T(8,128)(2,1)} %param.5, bf16[512,2048]{1,0:T(8,128)(2,1)} %param.4), kind=kOutput, calls=%fused_computation.55 | convolution fusion | flops 2148007936 | bytes 13107200 | tf_op jit(solution)/shard_map/dot_general | solution.py:81
  14.7 81.1 %collective-permute-done.1 = bf16[512,4096]{1,0:T(8,128)(2,1)} collective-permute-done((bf16[512,4096]{1,0:T(8,128)(2,1)}, bf16[512,4096]{1,0:T(8,128)(2,1)}, u32[]{:S(2)}, u32[]{:S(2)}) %collective-permute-start.1) | collective-permute-done | bytes 4194336 | tf_op jit(solution)/shard_map/ppermute | solution.py:14
  95.8 7.8 %fusion.44 = f32[512,4096]{1,0:T(8,128)} fusion(bf16[512,4096]{1,0:T(8,128)(2,1)} %collective-permute-done.1, bf16[512,2048]{1,0:T(8,128)(2,1)S(1)} %copy-done.3), kind=kOutput, calls=%fused_computation.57 | convolution fusion | flops 2147483648 | bytes 13107200 | tf_op jit(solution)/shard_map/dot_general | solution.py:89
  103.6 79.8 %collective-permute-done = bf16[512,4096]{1,0:T(8,128)(2,1)} collective-permute-done((bf16[512,4096]{1,0:T(8,128)(2,1)}, bf16[512,4096]{1,0:T(8,128)(2,1)}, u32[]{:S(2)}, u32[]{:S(2)}) %collective-permute-start) | collective-permute-done | bytes 4194336 | tf_op jit(solution)/shard_map/ppermute | solution.py:14
  183.4 7.8 %fusion.46 = f32[512,4096]{1,0:T(8,128)} fusion(bf16[512,4096]{1,0:T(8,128)(2,1)} %collective-permute-done, bf16[512,2048]{1,0:T(8,128)(2,1)S(1)} %copy-done.3), kind=kOutput, calls=%fused_computation.59 | convolution fusion | flops 2147483648 | bytes 13107200 | tf_op jit(solution)/shard_map/dot_general | solution.py:89
  191.1 83.2 %collective-permute-done.2 = bf16[512,4096]{1,0:T(8,128)(2,1)} collective-permute-done((bf16[512,4096]{1,0:T(8,128)(2,1)}, bf16[512,4096]{1,0:T(8,128)(2,1)}, u32[]{:S(2)}, u32[]{:S(2)}) %collective-permute-start.2) | collective-permute-done | bytes 4194336 | tf_op jit(solution)/shard_map/ppermute | solution.py:14
  274.3 10.0 %add_convert_fusion = bf16[512,4096]{1,0:T(8,128)(2,1)} fusion(f32[512,4096]{1,0:T(8,128)} %fusion.44, f32[512,4096]{1,0:T(8,128)S(1)} %fusion.41, f32[512,4096]{1,0:T(8,128)} %fusion.46, bf16[512,4096]{1,0:T(8,128)(2,1)} %collective-permute-done.2, pred[]{:T(512)S(6)} %and.117, pred[]{:T(512)S(6)} %and.116, pred[]{:T(512)S(6)} %and.115, ...), kind=kOutput, calls=%fused_computation | convolution fusion | flops 2162163712 | bytes 34078724 | tf_op jit(solution)/shard_map/dot_general | solution.py:89
  284.3 5.8 %all-to-all-start = ((bf16[2,256,4096]{2,1,0:T(8,128)(2,1)}), bf16[2,256,4096]{2,1,0:T(8,128)(2,1)}, u32[]{:S(2)}, u32[]{:S(2)}) async-start(bf16[2,256,4096]{2,1,0:T(8,128)(2,1)} %bitcast.126), calls=%async_computation | async-start | bytes 8388608 | tf_op jit(solution)/shard_map/all_to_all | solution.py:92
  293.4 23.0 %all-to-all-done = bf16[2,256,4096]{2,1,0:T(8,128)(2,1)} async-done(((bf16[2,256,4096]{2,1,0:T(8,128)(2,1)}), bf16[2,256,4096]{2,1,0:T(8,128)(2,1)}, u32[]{:S(2)}, u32[]{:S(2)}) %all-to-all-start) | async-done | bytes 4194336 | tf_op jit(solution)/shard_map/all_to_all | solution.py:92
  316.4 8.6 %copy.25 = bf16[256,2,4096]{2,1,0:T(2,128)(2,1)} copy(bf16[256,2,4096]{2,0,1:T(8,128)(2,1)} %bitcast.4) | data formatting | bytes 8388608 | tf_op jit(solution)/shard_map/all_to_all | solution.py:92
  325.0 8.2 %reshape.106 = bf16[128,2,64,128]{3,2,1,0:T(8,128)(2,1)} reshape(bf16[256,2,4096]{2,1,0:T(2,128)(2,1)} %copy.25) | data formatting | bytes 8388608 | tf_op jit(solution)/shard_map/reshape | solution.py:97
  333.2 3.2 fusion.30
  336.4 1.4 fusion.31
  337.9 1.5 convolution_subtract_fusion
  339.3 2.6 fusion
  341.9 5.2 %fusion.12 = f32[128,64,128]{2,0,1:T(8,128)S(1)} fusion(f32[128,64,128]{2,1,0:T(8,128)S(1)} %get-tuple-element.8), kind=kOutput, calls=%fused_computation.25 | convolution fusion | flops 805552128 | bytes 8388608 | tf_op jit(solution)/shard_map/rkn,nm->rkm/dot_general | solution.py:45
  347.2 5.4 %fusion.10 = f32[128,64,128]{2,0,1:T(8,128)S(1)} fusion(f32[128,64,128]{2,1,0:T(8,128)S(1)} %get-tuple-element.8), kind=kOutput, calls=%fused_computation.23 | convolution fusion | flops 805535744 | bytes 8388608 | tf_op jit(solution)/shard_map/rkn,nm->rkm/dot_general | solution.py:45
  352.6 5.3 %fusion.18 = f32[128,64,128]{2,0,1:T(8,128)S(1)} fusion(f32[128,64,128]{2,0,1:T(8,128)S(1)} %fusion.12, f32[128,64,128]{2,1,0:T(8,128)S(1)} %get-tuple-element.7), kind=kOutput, calls=%fused_computation.31 | convolution fusion | flops 806584320 | bytes 12582912 | tf_op jit(solution)/shard_map/rkn,nm->rkm/dot_general | solution.py:45
  358.0 6.1 %multiply_subtract_fusion.1 = (f32[128,64,128]{2,0,1:T(8,128)S(1)}, f32[128,64,128]{2,0,1:T(8,128)S(1)}) fusion(f32[128,64,128]{2,0,1:T(8,128)S(1)} %fusion.18, f32[64,128]{1,0:T(8,128)S(1)} %convolution_add_fusion.1, f32[64,128]{1,0:T(8,128)S(1)} %convolution_subtract_fusion.1, f32[128,64,128]{2,0,1:T(8,128)S(1)} %fusion.10, ...), kind=kOutput, calls=%fused_computation.14 | convolution fusion | flops 812892160 | bytes 21037056 | tf_op jit(solution)/shard_map/rkn,nm->rkm/dot_general | solution.py:45
  364.1 4.7 %fusion.2 = f32[128,64,128]{2,1,0:T(8,128)S(1)} fusion(f32[128,64,128]{2,0,1:T(8,128)S(1)} %get-tuple-element.6), kind=kOutput, calls=%fused_computation.15 | convolution fusion | flops 805535744 | bytes 8388608 | tf_op jit(solution)/shard_map/rkn,nm->rkm/dot_general | solution.py:45
  368.8 5.1 %fusion.4 = f32[128,64,128]{2,1,0:T(8,128)S(1)} fusion(f32[128,64,128]{2,0,1:T(8,128)S(1)} %get-tuple-element.6), kind=kOutput, calls=%fused_computation.17 | convolution fusion | flops 805552128 | bytes 8388608 | tf_op jit(solution)/shard_map/rkn,nm->rkm/dot_general | solution.py:45
  373.9 4.8 %fusion.27 = f32[128,64,128]{2,1,0:T(8,128)S(1)} fusion(f32[128,64,128]{2,1,0:T(8,128)S(1)} %fusion.2, f32[128,64,128]{2,0,1:T(8,128)S(1)} %get-tuple-element.5), kind=kOutput, calls=%fused_computation.34 | convolution fusion | flops 806600704 | bytes 12582912 | tf_op jit(solution)/shard_map/rkn,nm->rkm/dot_general | solution.py:45
  378.8 5.0 %fusion.24 = f32[128,64,128]{2,1,0:T(8,128)S(1)} fusion(f32[128,64,128]{2,1,0:T(8,128)S(1)} %fusion.4, f32[128,64,128]{2,0,1:T(8,128)S(1)} %get-tuple-element.5), kind=kOutput, calls=%fused_computation.33 | convolution fusion | flops 806584320 | bytes 12582912 | tf_op jit(solution)/shard_map/rkn,nm->rkm/dot_general | solution.py:45
  383.7 2.3 fusion.34
  386.1 2.3 fusion.35
  388.4 2.8 fusion.32
  391.2 2.8 fusion.33
  394.4 1.4 copy.36
  395.8 10.4 %copy.73 = bf16[32,8,64,128]{3,1,2,0:T(8,128)(2,1)} copy(bf16[32,8,64,128]{3,2,1,0:T(8,128)(2,1)S(1)} %bitcast.125) | data formatting | bytes 8388608
  (19 shorter events, 5.0 us)
Async XLA Ops:
  0.0 290.7 %copy-start = (f32[8192]{0:T(1024)S(1)}, f32[8192]{0:T(1024)}, u32[]{:S(2)}) copy-start(f32[8192]{0:T(1024)} %param.6) | copy-start | bytes 98308
  0.0 95.8 %collective-permute-start.1 = (bf16[512,4096]{1,0:T(8,128)(2,1)}, bf16[512,4096]{1,0:T(8,128)(2,1)}, u32[]{:S(2)}, u32[]{:S(2)}) collective-permute-start(bf16[512,4096]{1,0:T(8,128)(2,1)} %param.5), channel_id=1, source_target_pairs={{0,4},{2,6},{4,8},{6,10},{8,12},{10,14},{1,5},{3,7},{5,9},{7,11},{... | collective-permute-start | bytes 12582920 | tf_op jit(solution)/shard_map/ppermute | solution.py:14
  1.4 182.0 %collective-permute-start = (bf16[512,4096]{1,0:T(8,128)(2,1)}, bf16[512,4096]{1,0:T(8,128)(2,1)}, u32[]{:S(2)}, u32[]{:S(2)}) collective-permute-start(bf16[512,4096]{1,0:T(8,128)(2,1)} %param.5), channel_id=1, source_target_pairs={{0,2},{2,4},{4,6},{6,8},{8,10},{10,12},{12,14},{1,3},{3,5},{5,7},{... | collective-permute-start | bytes 12582920 | tf_op jit(solution)/shard_map/ppermute | solution.py:14
  3.4 270.9 %collective-permute-start.2 = (bf16[512,4096]{1,0:T(8,128)(2,1)}, bf16[512,4096]{1,0:T(8,128)(2,1)}, u32[]{:S(2)}, u32[]{:S(2)}) collective-permute-start(bf16[512,4096]{1,0:T(8,128)(2,1)} %param.5), channel_id=1, source_target_pairs={{0,6},{2,8},{4,10},{6,12},{8,14},{1,7},{3,9},{5,11},{7,13},{9,15},... | collective-permute-start | bytes 12582920 | tf_op jit(solution)/shard_map/ppermute | solution.py:14
  9.8 86.0 %copy-start.3 = (bf16[512,2048]{1,0:T(8,128)(2,1)S(1)}, bf16[512,2048]{1,0:T(8,128)(2,1)}, u32[]{:S(2)}) copy-start(bf16[512,2048]{1,0:T(8,128)(2,1)} %param.4) | copy-start | bytes 6291460
  284.3 32.1 %all-to-all-start = ((bf16[2,256,4096]{2,1,0:T(8,128)(2,1)}), bf16[2,256,4096]{2,1,0:T(8,128)(2,1)}, u32[]{:S(2)}, u32[]{:S(2)}) async-start(bf16[2,256,4096]{2,1,0:T(8,128)(2,1)} %bitcast.126), calls=%async_computation | async-start | bytes 8388608 | tf_op jit(solution)/shard_map/all_to_all | solution.py:92
  333.2 3.2 copy-start.2
  395.8 10.4 %copy-start.1 = (f32[8192]{0:T(1024)S(1)}, f32[8192]{0:T(1024)}, u32[]{:S(2)}) copy-start(f32[8192]{0:T(1024)} %param.6) | copy-start | bytes 98308
where the time goes:
time: 413 us; the launch traced here: 406 us
  waiting for transfers between devices  267 us (65%)
  matrix products  93.6 us (23%)
  local copies, waits for them, and re-layouts  30 us (7%)
  starting transfers between devices  10.5 us (3%)
  between operations  4.27 us (1%)
    ppermute x3, waiting for transfers between devices, shifted(): return lax.ppermute(block, axis, route)  244 us
    dot_general x12, matrix products, right_apply(): jnp.einsum('rkn,nm->rkm', values, table, precision=lax.Precision.HIGH)  43.8 us
    dot_general x3, matrix products, on_device(): product = jnp.dot(tile, previous, preferred_element_type=jnp.float32)  25.5 us
    all_to_all x1, waiting for transfers between devices, on_device(): lax.all_to_all(spatial, ('tm', 'rep'), split_axis=0, concat_axis=1, tiled...  23 us
    dot_general x10, matrix products, left_apply(): jnp.einsum('kn,rnm->rkm', table, values.astype(jnp.float32), precision=la...  19.5 us
    unnamed x9, local copies, waits for them, and re-layouts  10.4 us
    all_to_all x1, local copies, waits for them, and re-layouts, on_device(): lax.all_to_all(spatial, ('tm', 'rep'), split_axis=0, concat_axis=1, tiled...  8.6 us
  transfers between devices with their start and end apart: 4, of which 4 were waited for; matrix products, arithmetic and copies ran while one was open for 6% of the time, Pallas kernels for 0%

commit v1 on v0

--- a/solution.py
+++ b/solution.py
@@ -3,9 +3,15 @@
 import jax
 import jax.numpy as jnp
 from jax import lax
+from jax.experimental import pallas as pl
+from jax.experimental.pallas import tpu as pltpu
 from jax.sharding import PartitionSpec as P
 
 FIRST = 64
+CHUNK = 512
+TILE = 256
+AHEAD = 2
+MESH = pl.DeviceIdType.MESH
 
 
 def shifted(block, axis, distance):
@@ -107,10 +113,345 @@
     return joined.reshape(stations, days).astype(jnp.bfloat16)
 
 
+def sample_kernel(
+    factor, noise, time_kernel, regions, out,
+    weights, partial_weights, above, up_in, side_in, sibling, partial,
+    kept, given, got, toeplitz, acc,
+    up_send, up_recv, side_send, side_recv, sib_send, sib_recv, x_send, x_recv, tile_send, tile_recv,
+):
+    blocks = lax.axis_size("blk")
+    block = lax.axis_index("blk")
+    half = lax.axis_index("tm")
+    core = lax.rem(block, 2)
+    chip = lax.div(block, 2)
+    first_chip = chip == 0
+    last_chip = chip == blocks // 2 - 1
+    sib = block + 1 - 2 * core
+    width, local_days = noise.shape
+    chunks, _, chunk = up_in.shape
+    rows = width // 2
+    days = acc.shape[1]
+
+    def cols(step):
+        return pl.ds(pl.multiple_of(step * chunk, chunk), chunk)
+
+    def remote(src, dst, send, recv, where):
+        return pltpu.make_async_remote_copy(
+            src_ref=src, dst_ref=dst, send_sem=send, recv_sem=recv, device_id=where, device_id_type=MESH
+        )
+
+    def up_noise(step):
+        return remote(noise.at[:, cols(step)], up_in.at[step], up_send.at[step], up_recv.at[step], {"blk": block + 2})
+
+    def up_partial(step):
+        return remote(partial.at[step], up_in.at[step], up_send.at[step], up_recv.at[step], {"blk": block + 2})
+
+    def side(step):
+        return remote(up_in.at[step], side_in.at[step], side_send.at[step], side_recv.at[step], {"blk": sib})
+
+    def sib_copy(step):
+        return remote(noise.at[:, cols(step)], sibling.at[step], sib_send.at[step], sib_recv.at[step], {"blk": sib})
+
+    def cross(step):
+        return remote(given.at[step], got.at[step], x_send.at[step], x_recv.at[step], {"tm": 1 - half})
+
+    def tiles_down():
+        return remote(factor.at[:, pl.ds(2 * width, 2 * width)], above, tile_send, tile_recv, {"blk": block - 2})
+
+    barrier = pltpu.get_barrier_semaphore()
+    pl.semaphore_signal(barrier, inc=1, device_id={"blk": sib}, device_id_type=MESH)
+    pl.semaphore_signal(barrier, inc=1, device_id={"tm": 1 - half}, device_id_type=MESH)
+
+    @pl.when(jnp.logical_not(first_chip))
+    def _():
+        pl.semaphore_signal(barrier, inc=1, device_id={"blk": block - 2}, device_id_type=MESH)
+
+    @pl.when(jnp.logical_not(last_chip))
+    def _():
+        pl.semaphore_signal(barrier, inc=1, device_id={"blk": block + 2}, device_id_type=MESH)
+
+    pl.semaphore_wait(barrier, 2 + jnp.where(first_chip, 0, 1) + jnp.where(last_chip, 0, 1))
+
+    low = core == 0
+    high = core == 1
+    sends_up = jnp.logical_not(last_chip)
+    takes_up = jnp.logical_not(first_chip)
+
+    @pl.when(low & takes_up)
+    def _():
+        tiles_down().start()
+
+    @pl.when(high & sends_up)
+    def _():
+        for step in range(AHEAD):
+            up_noise(step).start()
+
+    @pl.when(low)
+    def _():
+        for step in range(AHEAD):
+            sib_copy(step).start()
+
+    def valid(index, back):
+        inside = index >= back
+        same = regions[jnp.maximum(index - back, 0)] == regions[index]
+        return jnp.where(inside & same, 1.0, 0.0).astype(jnp.float32)
+
+    v1, v2, v3 = valid(block, 1), valid(block, 2), valid(block, 3)
+    is_low = jnp.where(low, 1.0, 0.0).astype(jnp.float32)
+    is_high = 1.0 - is_low
+    strip = 64
+
+    def make_weights(index, carry):
+        at = pl.ds(pl.multiple_of(index * strip, strip), strip)
+        row = lax.broadcasted_iota(jnp.int32, (strip, width), 0) + index * strip
+        col = lax.broadcasted_iota(jnp.int32, (strip, width), 1)
+        t0, t1, t2, t3 = (factor[at, pl.ds(k * width, width)].astype(jnp.float32) for k in range(4))
+        eye = jnp.where(row == col, 1.0, 0.0)
+        near = v1 * t1
+        mid = v2 * t2
+        far = v3 * t3
+        first = is_low * (v3 * eye + (1.0 - v3) * mid) + is_high * mid
+        second = is_low * near + is_high * far
+        weights[at, pl.ds(0, width)] = jnp.where(row >= col, t0, 0.0).astype(jnp.bfloat16)
+        weights[at, pl.ds(width, width)] = (is_high * near).astype(jnp.bfloat16)
+        weights[at, pl.ds(2 * width, width)] = first.astype(jnp.bfloat16)
+        weights[at, pl.ds(3 * width, width)] = second.astype(jnp.bfloat16)
+        return carry
+
+    lax.fori_loop(0, width // strip, make_weights, 0)
+
+    line = jnp.broadcast_to(time_kernel[...], (16, days))
+    row_of = lax.broadcasted_iota(jnp.int32, (16, days), 0)
+    acc[pl.ds(0, 16), :] = line
+
+    def add_row(index, carry):
+        acc[pl.ds(0, 16), :] = jnp.where(row_of == index, pltpu.roll(line, index, 1), acc[pl.ds(0, 16), :])
+        return carry
+
+    lax.fori_loop(1, 16, add_row, 0)
+
+    def make_toeplitz(index, carry):
+        turned = pltpu.roll(acc[pl.ds(0, 16), :], index * 16, 1)
+        toeplitz[pl.ds(pl.multiple_of(index * 16, 16), 16), :] = turned.astype(jnp.bfloat16)
+        return carry
+
+    lax.fori_loop(0, TILE // 16, make_toeplitz, 0)
+
+    def clear(index, carry):
+        acc[:, pl.ds(pl.multiple_of(index * TILE, TILE), TILE)] = jnp.zeros((rows, TILE), jnp.float32)
+        return carry
+
+    lax.fori_loop(0, days // TILE, clear, 0)
+
+    @pl.when(low & sends_up)
+    def _():
+        tiles_down().wait_recv()
+        uses = valid(jnp.minimum(block + 2, blocks - 1), 3)
+
+        def make_partial_weights(index, carry):
+            at = pl.ds(pl.multiple_of(index * strip, strip), strip)
+            row = lax.broadcasted_iota(jnp.int32, (strip, width), 0) + index * strip
+            col = lax.broadcasted_iota(jnp.int32, (strip, width), 1)
+            t2, t3 = (above[at, pl.ds(k * width, width)].astype(jnp.float32) for k in range(2))
+            eye = jnp.where(row == col, 1.0, 0.0)
+            partial_weights[at, pl.ds(0, width)] = (uses * t2 + (1.0 - uses) * eye).astype(jnp.bfloat16)
+            partial_weights[at, pl.ds(width, width)] = (uses * t3).astype(jnp.bfloat16)
+            return carry
+
+        lax.fori_loop(0, width // strip, make_partial_weights, 0)
+
+    def dot(left, right):
+        return jnp.dot(left, right, preferred_element_type=jnp.float32)
+
+    def send_stage(step):
+        nothing = jnp.zeros((width, chunk), jnp.bfloat16)
+
+        @pl.when(high & sends_up & (step + AHEAD < chunks))
+        def _():
+            up_noise(step).wait_send()
+            up_noise(step + AHEAD).start()
+
+        @pl.when(low & (step + AHEAD < chunks))
+        def _():
+            sib_copy(step + AHEAD).start()
+
+        @pl.when(high & takes_up)
+        def _():
+            up_noise(step).wait_recv()
+            side(step).start()
+
+        @pl.when(low & takes_up)
+        def _():
+            side(step).wait_recv()
+
+        @pl.when(first_chip)
+        def _():
+            side_in[step] = nothing
+            up_in[step] = nothing
+
+        @pl.when(low)
+        def _():
+            sibling[step] = nothing
+
+        @pl.when(low & sends_up)
+        def _():
+            for part in range(0, width, rows):
+                at = pl.ds(part, rows)
+                total = dot(partial_weights[at, pl.ds(0, width)], noise[:, cols(step)])
+                total += dot(partial_weights[at, pl.ds(width, width)], side_in[step])
+                partial[step, at, :] = total.astype(jnp.bfloat16)
+            up_partial(step).start()
+
+    def spatial(step, at):
+        total = dot(weights[at, pl.ds(0, width)], noise[:, cols(step)])
+        total += dot(weights[at, pl.ds(width, width)], sibling[step])
+        total += dot(weights[at, pl.ds(2 * width, width)], up_in[step])
+        total += dot(weights[at, pl.ds(3 * width, width)], side_in[step])
+        return total.astype(jnp.bfloat16)
+
+    def mix_stage(step):
+        @pl.when(low & takes_up)
+        def _():
+            up_partial(step).wait_recv()
+            side(step).start()
+
+        @pl.when(high & takes_up)
+        def _():
+            side(step).wait_recv()
+
+        @pl.when(high)
+        def _():
+            sib_copy(step).wait_recv()
+
+        given[step] = spatial(step, pl.ds(pl.multiple_of((1 - half) * rows, rows), rows))
+        cross(step).start()
+        kept[step] = spatial(step, pl.ds(pl.multiple_of(half * rows, rows), rows))
+
+    def filter_stage(step):
+        cross(step).wait_recv()
+        mine = half * local_days + step * chunk
+        other = (1 - half) * local_days + step * chunk
+
+        def one(index, carry):
+            at = index * TILE
+            parts = []
+            for start in (mine, other):
+                for piece in range(0, chunk, TILE):
+                    offset = lax.rem(at - start - piece + days, days)
+                    parts.append(toeplitz[:, pl.ds(pl.multiple_of(offset, TILE), TILE)])
+            left = jnp.concatenate([kept[step], got[step]], axis=1)
+            right = jnp.concatenate(parts, axis=0)
+            acc[:, pl.ds(pl.multiple_of(at, TILE), TILE)] += dot(left, right)
+            return carry
+
+        lax.fori_loop(0, days // TILE, one, 0, unroll=4)
+
+    def body(turn, carry):
+        @pl.when(turn < chunks)
+        def _():
+            send_stage(turn)
+
+        @pl.when((turn >= 1) & (turn <= chunks))
+        def _():
+            mix_stage(turn - 1)
+
+        @pl.when(turn >= 2)
+        def _():
+            filter_stage(turn - 2)
+
+        return carry
+
+    lax.fori_loop(0, chunks + 2, body, 0)
+
+    def finish(index, carry):
+        at = pl.ds(pl.multiple_of(index * TILE, TILE), TILE)
+        out[:, at] = acc[:, at].astype(jnp.bfloat16)
+        return carry
+
+    lax.fori_loop(0, days // TILE, finish, 0)
+
+    def drain(step, carry):
+        cross(step).wait_send()
+
+        @pl.when(takes_up)
+        def _():
+            side(step).wait_send()
+
+        @pl.when(low)
+        def _():
+            sib_copy(step).wait_send()
+
+        @pl.when(low & sends_up)
+        def _():
+            up_partial(step).wait_send()
+
+        @pl.when(high & sends_up & (step + AHEAD >= chunks))
+        def _():
+            up_noise(step).wait_send()
+
+        return carry
+
+    lax.fori_loop(0, chunks, drain, 0)
+
+    @pl.when(low & takes_up)
+    def _():
+        tiles_down().wait_send()
+
+
+def fused(factor_rows, noise, time_kernel, region_of_block):
+    width, local_days = noise.shape
+    days = time_kernel.shape[0]
+    chunks = local_days // CHUNK
+    rows = width // 2
+    vmem = pl.BlockSpec(memory_space=pltpu.VMEM)
+    half = jnp.bfloat16
+    pair = [pltpu.SemaphoreType.DMA((chunks,))] * 2
+    return pl.pallas_call(
+        sample_kernel,
+        out_shape=jax.ShapeDtypeStruct((rows, days), half),
+        in_specs=[vmem, vmem, vmem, pl.BlockSpec(memory_space=pltpu.SMEM)],
+        out_specs=vmem,
+        scratch_shapes=[
+            pltpu.VMEM((width, 4 * width), half),
+            pltpu.VMEM((width, 2 * width), half),
+            pltpu.VMEM((width, 2 * width), half),
+            pltpu.VMEM((chunks, width, CHUNK), half),
+            pltpu.VMEM((chunks, width, CHUNK), half),
+            pltpu.VMEM((chunks, width, CHUNK), half),
+            pltpu.VMEM((chunks, width, CHUNK), half),
+            pltpu.VMEM((chunks, rows, CHUNK), half),
+            pltpu.VMEM((chunks, rows, CHUNK), half),
+            pltpu.VMEM((chunks, rows, CHUNK), half),
+            pltpu.VMEM((TILE, days), half),
+            pltpu.VMEM((rows, days), jnp.float32),
+        ]
+        + pair * 4
+        + [pltpu.SemaphoreType.DMA, pltpu.SemaphoreType.DMA],
+        compiler_params=pltpu.CompilerParams(
+            collective_id=0, has_side_effects=True, vmem_limit_bytes=60 * 1024 * 1024
+        ),
+        cost_estimate=pl.CostEstimate(
+            flops=2 * rows * days * days + 8 * width * width * local_days,
+            bytes_accessed=4 * width * local_days + 8 * width * width,
+            transcendentals=0,
+        ),
+    )(factor_rows, noise, time_kernel.reshape(1, days), region_of_block)
+
+
 def solution(mesh):
     placed = (P(("grp", "blk"), None), P(("grp", "blk"), ("tm", "rep")), P(), P("grp"))
+    sizes = dict(mesh.shape)
+    paired = sizes["tm"] == 2 and sizes["rep"] == 1 and sizes["blk"] % 2 == 0
+
+    def program(factor_rows, noise, time_kernel, region_of_block):
+        width, local_days = noise.shape
+        fits = width == 2 * TILE and factor_rows.shape[1] == 4 * width
+        fits = fits and local_days % CHUNK == 0 and local_days >= AHEAD * CHUNK
+        run = fused if paired and fits else on_device
+        return run(factor_rows, noise, time_kernel, region_of_block)
+
     return jax.shard_map(
-        on_device,
+        program,
         mesh=mesh,
         in_specs=placed,
         out_specs=P(("grp", "blk", "tm", "rep"), None),

time: 413 us -> 137 us (0.33)
  the two profiles are of different devices: /device:TPU:24 before, /device:TPU:9 now
where the time goes in v1:
time: 137 us
  Pallas kernels  132 us (96%)
  local copies, waits for them, and re-layouts  4.64 us (3%)
    pallas_call x1, Pallas kernels, fused(): pl.pallas_call(sample_kernel, out_shape=jax.ShapeDtypeStruct((rows, days)...  132 us
    unnamed x1, local copies, waits for them, and re-layouts  4.64 us

profile of v1, /device:TPU:9, one launch (start us, length us, event | category | flops | bytes accessed | tf_op | source)
XLA Modules:
  0.0 137.1 jit_solution(1184685287695192738)
XLA Ops:
  0.0 132.5 %shard_map.46 = bf16[256,8192]{1,0:T(8,128)(2,1)} custom-call(bf16[512,2048]{1,0:T(8,128)(2,1)} %factor.1, bf16[512,4096]{1,0:T(8,128)(2,1)} %noise.1, f32[1,8192]{1,0:T(1,128)} %bitcast.1, s32[8]{0:T(128)} %regions.1), custom_call_target="tpu_custom_call" | custom-call | flops 42949672960 | bytes 10485760 | tf_op jit(solution)/shard_map/pallas_call | solution.py:409
  132.5 4.6 %copy.6 = bf16[256,8192]{1,0:T(8,128)(2,1)} copy(bf16[256,8192]{1,0:T(8,128)(2,1)} %shard_map.46) | data formatting | bytes 8388608

commit v2 on v1

--- a/solution.py
+++ b/solution.py
@@ -8,9 +8,10 @@
 from jax.sharding import PartitionSpec as P
 
 FIRST = 64
-CHUNK = 512
+CHUNK = 256
 TILE = 256
-AHEAD = 2
+AHEAD = 6
+LEAD = 3
 MESH = pl.DeviceIdType.MESH
 
 
@@ -116,7 +117,7 @@
 def sample_kernel(
     factor, noise, time_kernel, regions, out,
     weights, partial_weights, above, up_in, side_in, sibling, partial,
-    kept, given, got, toeplitz, acc,
+    kept, given, got, toeplitz_sum, toeplitz_diff, acc,
     up_send, up_recv, side_send, side_recv, sib_send, sib_recv, x_send, x_recv, tile_send, tile_recv,
 ):
     blocks = lax.axis_size("blk")
@@ -220,22 +221,32 @@
 
     lax.fori_loop(0, width // strip, make_weights, 0)
 
-    line = jnp.broadcast_to(time_kernel[...], (16, days))
-    row_of = lax.broadcasted_iota(jnp.int32, (16, days), 0)
-    acc[pl.ds(0, 16), :] = line
-
-    def add_row(index, carry):
-        acc[pl.ds(0, 16), :] = jnp.where(row_of == index, pltpu.roll(line, index, 1), acc[pl.ds(0, 16), :])
-        return carry
-
-    lax.fori_loop(1, 16, add_row, 0)
-
-    def make_toeplitz(index, carry):
-        turned = pltpu.roll(acc[pl.ds(0, 16), :], index * 16, 1)
-        toeplitz[pl.ds(pl.multiple_of(index * 16, 16), 16), :] = turned.astype(jnp.bfloat16)
-        return carry
-
-    lax.fori_loop(0, TILE // 16, make_toeplitz, 0)
+    def make_toeplitz(line, target):
+        length = line.shape[1]
+        wide = jnp.broadcast_to(line, (8, length))
+        row_of = lax.broadcasted_iota(jnp.int32, (8, length), 0)
+        base = acc.at[pl.ds(0, 8), pl.ds(0, length)]
+        base[...] = wide
+
+        def add_row(index, carry):
+            base[...] = jnp.where(row_of == index, pltpu.roll(wide, index, 1), base[...])
+            return carry
+
+        lax.fori_loop(1, 8, add_row, 0)
+
+        def add_strip(index, carry):
+            upper = pltpu.roll(base[...], index * 16, 1)
+            lower = pltpu.roll(base[...], index * 16 + 8, 1)
+            both = jnp.concatenate([upper, lower], axis=0)
+            target[pl.ds(pl.multiple_of(index * 16, 16), 16), :] = both.astype(jnp.bfloat16)
+            return carry
+
+        lax.fori_loop(0, TILE // 16, add_strip, 0)
+
+    early, late = time_kernel[:, pl.ds(0, days // 2)], time_kernel[:, pl.ds(days // 2, days // 2)]
+    make_toeplitz(0.5 * (early + late), toeplitz_sum)
+    difference = 0.5 * (early - late)
+    make_toeplitz(jnp.concatenate([difference, -difference], axis=1), toeplitz_diff)
 
     def clear(index, carry):
         acc[:, pl.ds(pl.multiple_of(index * TILE, TILE), TILE)] = jnp.zeros((rows, TILE), jnp.float32)
@@ -329,46 +340,53 @@
 
     def filter_stage(step):
         cross(step).wait_recv()
-        mine = half * local_days + step * chunk
-        other = (1 - half) * local_days + step * chunk
+        first = kept[step].astype(jnp.float32)
+        second = got[step].astype(jnp.float32)
+        sign = jnp.where(half == 0, 1.0, -1.0).astype(jnp.float32)
+        total = (first + second).astype(jnp.bfloat16)
+        difference = (sign * (first - second)).astype(jnp.bfloat16)
+        start = step * chunk
 
         def one(index, carry):
             at = index * TILE
-            parts = []
-            for start in (mine, other):
-                for piece in range(0, chunk, TILE):
-                    offset = lax.rem(at - start - piece + days, days)
-                    parts.append(toeplitz[:, pl.ds(pl.multiple_of(offset, TILE), TILE)])
-            left = jnp.concatenate([kept[step], got[step]], axis=1)
-            right = jnp.concatenate(parts, axis=0)
-            acc[:, pl.ds(pl.multiple_of(at, TILE), TILE)] += dot(left, right)
+            sums, diffs = [], []
+            for piece in range(0, chunk, TILE):
+                offset = lax.rem(at - start - piece + days, days)
+                folded = lax.rem(offset, days // 2)
+                sums.append(toeplitz_sum[:, pl.ds(pl.multiple_of(folded, TILE), TILE)])
+                diffs.append(toeplitz_diff[:, pl.ds(pl.multiple_of(offset, TILE), TILE)])
+            acc[:, pl.ds(pl.multiple_of(at, TILE), TILE)] += dot(total, jnp.concatenate(sums, axis=0))
+            acc[:, pl.ds(pl.multiple_of(at + days // 2, TILE), TILE)] += dot(difference, jnp.concatenate(diffs, axis=0))
             return carry
 
-        lax.fori_loop(0, days // TILE, one, 0, unroll=4)
+        lax.fori_loop(0, days // 2 // TILE, one, 0, unroll=4)
 
     def body(turn, carry):
         @pl.when(turn < chunks)
         def _():
             send_stage(turn)
 
-        @pl.when((turn >= 1) & (turn <= chunks))
-        def _():
-            mix_stage(turn - 1)
-
-        @pl.when(turn >= 2)
-        def _():
-            filter_stage(turn - 2)
+        @pl.when((turn >= LEAD) & (turn < chunks + LEAD))
+        def _():
+            mix_stage(turn - LEAD)
+
+        @pl.when(turn >= LEAD + 1)
+        def _():
+            filter_stage(turn - LEAD - 1)
 
         return carry
 
-    lax.fori_loop(0, chunks + 2, body, 0)
+    lax.fori_loop(0, chunks + LEAD + 1, body, 0)
 
     def finish(index, carry):
-        at = pl.ds(pl.multiple_of(index * TILE, TILE), TILE)
-        out[:, at] = acc[:, at].astype(jnp.bfloat16)
+        low_at = pl.ds(pl.multiple_of(index * TILE, TILE), TILE)
+        high_at = pl.ds(pl.multiple_of(index * TILE + days // 2, TILE), TILE)
+        sums, diffs = acc[:, low_at], acc[:, high_at]
+        out[:, low_at] = (sums + diffs).astype(jnp.bfloat16)
+        out[:, high_at] = (sums - diffs).astype(jnp.bfloat16)
         return carry
 
-    lax.fori_loop(0, days // TILE, finish, 0)
+    lax.fori_loop(0, days // 2 // TILE, finish, 0)
 
     def drain(step, carry):
         cross(step).wait_send()
@@ -422,6 +440,7 @@
             pltpu.VMEM((chunks, rows, CHUNK), half),
             pltpu.VMEM((chunks, rows, CHUNK), half),
             pltpu.VMEM((chunks, rows, CHUNK), half),
+            pltpu.VMEM((TILE, days // 2), half),
             pltpu.VMEM((TILE, days), half),
             pltpu.VMEM((rows, days), jnp.float32),
         ]
@@ -431,7 +450,7 @@
             collective_id=0, has_side_effects=True, vmem_limit_bytes=60 * 1024 * 1024
         ),
         cost_estimate=pl.CostEstimate(
-            flops=2 * rows * days * days + 8 * width * width * local_days,
+            flops=rows * days * days + 8 * width * width * local_days,
             bytes_accessed=4 * width * local_days + 8 * width * width,
             transcendentals=0,
         ),
@@ -446,7 +465,7 @@
     def program(factor_rows, noise, time_kernel, region_of_block):
         width, local_days = noise.shape
         fits = width == 2 * TILE and factor_rows.shape[1] == 4 * width
-        fits = fits and local_days % CHUNK == 0 and local_days >= AHEAD * CHUNK
+        fits = fits and 2 * local_days == time_kernel.shape[0] and local_days % CHUNK == 0 and local_days >= AHEAD * CHUNK
         run = fused if paired and fits else on_device
         return run(factor_rows, noise, time_kernel, region_of_block)
 

time: 137 us -> 135 us (0.985)
  Pallas kernels: 132 us -> 130 us
    pallas_call x1, Pallas kernels: 132 us -> 130 us  [fused(): pl.pallas_call(sample_kernel, out_shape=jax.ShapeDtypeStruct((rows, days)...]
where the time goes in v2:
time: 135 us
  Pallas kernels  130 us (96%)
  local copies, waits for them, and re-layouts  4.64 us (3%)
    pallas_call x1, Pallas kernels, fused(): pl.pallas_call(sample_kernel, out_shape=jax.ShapeDtypeStruct((rows, days)...  130 us
    unnamed x1, local copies, waits for them, and re-layouts  4.64 us

profile of v2, /device:TPU:9, one launch (start us, length us, event | category | flops | bytes accessed | tf_op | source)
XLA Modules:
  0.0 134.9 jit_solution(9253869551818144776)
XLA Ops:
  0.0 130.3 %shard_map.46 = bf16[256,8192]{1,0:T(8,128)(2,1)} custom-call(bf16[512,2048]{1,0:T(8,128)(2,1)} %factor.1, bf16[512,4096]{1,0:T(8,128)(2,1)} %noise.1, f32[1,8192]{1,0:T(1,128)} %bitcast.1, s32[8]{0:T(128)} %regions.1), custom_call_target="tpu_custom_call" | custom-call | flops 25769803776 | bytes 10485760 | tf_op jit(solution)/shard_map/pallas_call | solution.py:427
  130.3 4.6 %copy.6 = bf16[256,8192]{1,0:T(8,128)(2,1)} copy(bf16[256,8192]{1,0:T(8,128)(2,1)} %shard_map.46) | data formatting | bytes 8388608

commit v3 on v2

--- a/solution.py
+++ b/solution.py
@@ -11,7 +11,8 @@
 CHUNK = 256
 TILE = 256
 AHEAD = 6
-LEAD = 3
+LAG = 2
+LEAD = 4
 MESH = pl.DeviceIdType.MESH
 
 
@@ -115,10 +116,10 @@
 
 
 def sample_kernel(
-    factor, noise, time_kernel, regions, out,
-    weights, partial_weights, above, up_in, side_in, sibling, partial,
+    factor_hbm, noise_hbm, time_kernel, regions, out,
+    factor, noise, staged, weights, partial_weights, above, up_in, side_in, shared,
     kept, given, got, toeplitz_sum, toeplitz_diff, acc,
-    up_send, up_recv, side_send, side_recv, sib_send, sib_recv, x_send, x_recv, tile_send, tile_recv,
+    up_send, up_recv, side_send, side_recv, sib_send, sib_recv, x_send, x_recv, out_sem, tile_send, tile_recv, factor_sem, noise_sem,
 ):
     blocks = lax.axis_size("blk")
     block = lax.axis_index("blk")
@@ -142,23 +143,26 @@
         )
 
     def up_noise(step):
-        return remote(noise.at[:, cols(step)], up_in.at[step], up_send.at[step], up_recv.at[step], {"blk": block + 2})
+        return remote(noise_hbm.at[:, cols(step)], up_in.at[step], up_send.at[step], up_recv.at[step], {"blk": block + 2})
 
     def up_partial(step):
-        return remote(partial.at[step], up_in.at[step], up_send.at[step], up_recv.at[step], {"blk": block + 2})
+        return remote(shared.at[step], up_in.at[step], up_send.at[step], up_recv.at[step], {"blk": block + 2})
 
     def side(step):
         return remote(up_in.at[step], side_in.at[step], side_send.at[step], side_recv.at[step], {"blk": sib})
 
     def sib_copy(step):
-        return remote(noise.at[:, cols(step)], sibling.at[step], sib_send.at[step], sib_recv.at[step], {"blk": sib})
+        return remote(noise_hbm.at[:, cols(step)], shared.at[step], sib_send.at[step], sib_recv.at[step], {"blk": sib})
 
     def cross(step):
         return remote(given.at[step], got.at[step], x_send.at[step], x_recv.at[step], {"tm": 1 - half})
 
     def tiles_down():
-        return remote(factor.at[:, pl.ds(2 * width, 2 * width)], above, tile_send, tile_recv, {"blk": block - 2})
-
+        return remote(factor_hbm.at[:, pl.ds(2 * width, 2 * width)], above, tile_send, tile_recv, {"blk": block - 2})
+
+    load_factor = pltpu.make_async_copy(factor_hbm, factor, factor_sem)
+    load_noise = pltpu.make_async_copy(noise_hbm, noise, noise_sem)
+    load_factor.start()
     barrier = pltpu.get_barrier_semaphore()
     pl.semaphore_signal(barrier, inc=1, device_id={"blk": sib}, device_id_type=MESH)
     pl.semaphore_signal(barrier, inc=1, device_id={"tm": 1 - half}, device_id_type=MESH)
@@ -191,6 +195,8 @@
     def _():
         for step in range(AHEAD):
             sib_copy(step).start()
+
+    load_noise.start()
 
     def valid(index, back):
         inside = index >= back
@@ -219,6 +225,7 @@
         weights[at, pl.ds(3 * width, width)] = second.astype(jnp.bfloat16)
         return carry
 
+    load_factor.wait()
     lax.fori_loop(0, width // strip, make_weights, 0)
 
     def make_toeplitz(line, target):
@@ -271,6 +278,8 @@
 
         lax.fori_loop(0, width // strip, make_partial_weights, 0)
 
+    load_noise.wait()
+
     def dot(left, right):
         return jnp.dot(left, right, preferred_element_type=jnp.float32)
 
@@ -291,18 +300,15 @@
             up_noise(step).wait_recv()
             side(step).start()
 
-        @pl.when(low & takes_up)
-        def _():
-            side(step).wait_recv()
-
         @pl.when(first_chip)
         def _():
             side_in[step] = nothing
             up_in[step] = nothing
 
-        @pl.when(low)
-        def _():
-            sibling[step] = nothing
+    def partial_stage(step):
+        @pl.when(low & takes_up)
+        def _():
+            side(step).wait_recv()
 
         @pl.when(low & sends_up)
         def _():
@@ -310,12 +316,13 @@
                 at = pl.ds(part, rows)
                 total = dot(partial_weights[at, pl.ds(0, width)], noise[:, cols(step)])
                 total += dot(partial_weights[at, pl.ds(width, width)], side_in[step])
-                partial[step, at, :] = total.astype(jnp.bfloat16)
+                shared[step, at, :] = total.astype(jnp.bfloat16)
             up_partial(step).start()
 
-    def spatial(step, at):
+    def spatial(step, at, with_sibling):
         total = dot(weights[at, pl.ds(0, width)], noise[:, cols(step)])
-        total += dot(weights[at, pl.ds(width, width)], sibling[step])
+        if with_sibling:
+            total += dot(weights[at, pl.ds(width, width)], shared[step])
         total += dot(weights[at, pl.ds(2 * width, width)], up_in[step])
         total += dot(weights[at, pl.ds(3 * width, width)], side_in[step])
         return total.astype(jnp.bfloat16)
@@ -334,11 +341,16 @@
         def _():
             sib_copy(step).wait_recv()
 
-        given[step] = spatial(step, pl.ds(pl.multiple_of((1 - half) * rows, rows), rows))
-        cross(step).start()
-        kept[step] = spatial(step, pl.ds(pl.multiple_of(half * rows, rows), rows))
-
-    def filter_stage(step):
+        send_rows = pl.ds(pl.multiple_of((1 - half) * rows, rows), rows)
+        keep_rows = pl.ds(pl.multiple_of(half * rows, rows), rows)
+        for chosen, with_sibling in ((low, False), (high, True)):
+            @pl.when(chosen)
+            def _():
+                given[step] = spatial(step, send_rows, with_sibling)
+                cross(step).start()
+                kept[step] = spatial(step, keep_rows, with_sibling)
+
+    def filter_stage(step, last):
         cross(step).wait_recv()
         first = kept[step].astype(jnp.float32)
         second = got[step].astype(jnp.float32)
@@ -355,8 +367,18 @@
                 folded = lax.rem(offset, days // 2)
                 sums.append(toeplitz_sum[:, pl.ds(pl.multiple_of(folded, TILE), TILE)])
                 diffs.append(toeplitz_diff[:, pl.ds(pl.multiple_of(offset, TILE), TILE)])
-            acc[:, pl.ds(pl.multiple_of(at, TILE), TILE)] += dot(total, jnp.concatenate(sums, axis=0))
-            acc[:, pl.ds(pl.multiple_of(at + days // 2, TILE), TILE)] += dot(difference, jnp.concatenate(diffs, axis=0))
+            low_at = pl.ds(pl.multiple_of(at, TILE), TILE)
+            high_at = pl.ds(pl.multiple_of(at + days // 2, TILE), TILE)
+            sum_part = acc[:, low_at] + dot(total, jnp.concatenate(sums, axis=0))
+            diff_part = acc[:, high_at] + dot(difference, jnp.concatenate(diffs, axis=0))
+            if last:
+                staged[:, low_at] = (sum_part + diff_part).astype(jnp.bfloat16)
+                staged[:, high_at] = (sum_part - diff_part).astype(jnp.bfloat16)
+                pltpu.make_async_copy(staged.at[:, low_at], out.at[:, low_at], out_sem.at[2 * index]).start()
+                pltpu.make_async_copy(staged.at[:, high_at], out.at[:, high_at], out_sem.at[2 * index + 1]).start()
+            else:
+                acc[:, low_at] = sum_part
+                acc[:, high_at] = diff_part
             return carry
 
         lax.fori_loop(0, days // 2 // TILE, one, 0, unroll=4)
@@ -366,27 +388,22 @@
         def _():
             send_stage(turn)
 
+        @pl.when((turn >= LAG) & (turn < chunks + LAG))
+        def _():
+            partial_stage(turn - LAG)
+
         @pl.when((turn >= LEAD) & (turn < chunks + LEAD))
         def _():
             mix_stage(turn - LEAD)
 
         @pl.when(turn >= LEAD + 1)
         def _():
-            filter_stage(turn - LEAD - 1)
+            filter_stage(turn - LEAD - 1, False)
 
         return carry
 
-    lax.fori_loop(0, chunks + LEAD + 1, body, 0)
-
-    def finish(index, carry):
-        low_at = pl.ds(pl.multiple_of(index * TILE, TILE), TILE)
-        high_at = pl.ds(pl.multiple_of(index * TILE + days // 2, TILE), TILE)
-        sums, diffs = acc[:, low_at], acc[:, high_at]
-        out[:, low_at] = (sums + diffs).astype(jnp.bfloat16)
-        out[:, high_at] = (sums - diffs).astype(jnp.bfloat16)
-        return carry
-
-    lax.fori_loop(0, days // 2 // TILE, finish, 0)
+    lax.fori_loop(0, chunks + LEAD, body, 0)
+    filter_stage(chunks - 1, True)
 
     def drain(step, carry):
         cross(step).wait_send()
@@ -414,6 +431,11 @@
     @pl.when(low & takes_up)
     def _():
         tiles_down().wait_send()
+
+    for index in range(days // TILE):
+        half_tiles = days // 2 // TILE
+        at = pl.ds((index // 2 + index % 2 * half_tiles) * TILE, TILE)
+        pltpu.make_async_copy(staged.at[:, at], out.at[:, at], out_sem.at[index]).wait()
 
 
 def fused(factor_rows, noise, time_kernel, region_of_block):
@@ -422,18 +444,21 @@
     chunks = local_days // CHUNK
     rows = width // 2
     vmem = pl.BlockSpec(memory_space=pltpu.VMEM)
+    hbm = pl.BlockSpec(memory_space=pl.ANY)
     half = jnp.bfloat16
     pair = [pltpu.SemaphoreType.DMA((chunks,))] * 2
     return pl.pallas_call(
         sample_kernel,
         out_shape=jax.ShapeDtypeStruct((rows, days), half),
-        in_specs=[vmem, vmem, vmem, pl.BlockSpec(memory_space=pltpu.SMEM)],
-        out_specs=vmem,
+        in_specs=[hbm, hbm, vmem, pl.BlockSpec(memory_space=pltpu.SMEM)],
+        out_specs=hbm,
         scratch_shapes=[
+            pltpu.VMEM((width, 4 * width), half),
+            pltpu.VMEM((width, local_days), half),
+            pltpu.VMEM((rows, days), half),
             pltpu.VMEM((width, 4 * width), half),
             pltpu.VMEM((width, 2 * width), half),
             pltpu.VMEM((width, 2 * width), half),
-            pltpu.VMEM((chunks, width, CHUNK), half),
             pltpu.VMEM((chunks, width, CHUNK), half),
             pltpu.VMEM((chunks, width, CHUNK), half),
             pltpu.VMEM((chunks, width, CHUNK), half),
@@ -445,7 +470,8 @@
             pltpu.VMEM((rows, days), jnp.float32),
         ]
         + pair * 4
-        + [pltpu.SemaphoreType.DMA, pltpu.SemaphoreType.DMA],
+        + [pltpu.SemaphoreType.DMA((days // TILE,))]
+        + [pltpu.SemaphoreType.DMA] * 4,
         compiler_params=pltpu.CompilerParams(
             collective_id=0, has_side_effects=True, vmem_limit_bytes=60 * 1024 * 1024
         ),

time: 135 us -> 115 us (0.85)
  Pallas kernels: 130 us -> 110 us
    pallas_call x1, Pallas kernels: 130 us -> 110 us  [fused(): pl.pallas_call(sample_kernel, out_shape=jax.ShapeDtypeStruct((rows, days)...]
where the time goes in v3:
time: 115 us
  Pallas kernels  110 us (96%)
  local copies, waits for them, and re-layouts  4.64 us (4%)
    pallas_call x1, Pallas kernels, fused(): pl.pallas_call(sample_kernel, out_shape=jax.ShapeDtypeStruct((rows, days)...  110 us
    unnamed x1, local copies, waits for them, and re-layouts  4.64 us

profile of v3, /device:TPU:9, one launch (start us, length us, event | category | flops | bytes accessed | tf_op | source)
XLA Modules:
  0.0 114.9 jit_solution(10497251977884945383)
XLA Ops:
  0.0 110.2 %shard_map.46 = bf16[256,8192]{1,0:T(8,128)(2,1)} custom-call(bf16[512,2048]{1,0:T(8,128)(2,1)} %factor_hbm.1, bf16[512,4096]{1,0:T(8,128)(2,1)} %noise_hbm.1, f32[1,8192]{1,0:T(1,128)} %bitcast.1, s32[8]{0:T(128)} %regions.1), custom_call_target="tpu_custom_call" | custom-call | flops 25769803776 | bytes 10485760 | tf_op jit(solution)/shard_map/pallas_call | solution.py:450
  110.2 4.6 %copy.6 = bf16[256,8192]{1,0:T(8,128)(2,1)} copy(bf16[256,8192]{1,0:T(8,128)(2,1)} %shard_map.46) | data formatting | bytes 8388608

commit v4 on v3

--- a/solution.py
+++ b/solution.py
@@ -117,9 +117,9 @@
 
 def sample_kernel(
     factor_hbm, noise_hbm, time_kernel, regions, out,
-    factor, noise, staged, weights, partial_weights, above, up_in, side_in, shared,
+    factor, noise, weights, partial_weights, above, up_in, side_in, shared,
     kept, given, got, toeplitz_sum, toeplitz_diff, acc,
-    up_send, up_recv, side_send, side_recv, sib_send, sib_recv, x_send, x_recv, out_sem, tile_send, tile_recv, factor_sem, noise_sem,
+    up_send, up_recv, side_send, side_recv, sib_send, sib_recv, x_send, x_recv, tile_send, tile_recv, factor_sem, noise_sem,
 ):
     blocks = lax.axis_size("blk")
     block = lax.axis_index("blk")
@@ -350,20 +350,23 @@
                 cross(step).start()
                 kept[step] = spatial(step, keep_rows, with_sibling)
 
-    def filter_stage(step, last):
-        cross(step).wait_recv()
-        first = kept[step].astype(jnp.float32)
-        second = got[step].astype(jnp.float32)
+    def filter_stage(steps, last):
         sign = jnp.where(half == 0, 1.0, -1.0).astype(jnp.float32)
-        total = (first + second).astype(jnp.bfloat16)
-        difference = (sign * (first - second)).astype(jnp.bfloat16)
-        start = step * chunk
+        totals, differences = [], []
+        for step in steps:
+            cross(step).wait_recv()
+            first = kept[step].astype(jnp.float32)
+            second = got[step].astype(jnp.float32)
+            totals.append((first + second).astype(jnp.bfloat16))
+            differences.append((sign * (first - second)).astype(jnp.bfloat16))
+        total = jnp.concatenate(totals, axis=1)
+        difference = jnp.concatenate(differences, axis=1)
 
         def one(index, carry):
             at = index * TILE
             sums, diffs = [], []
-            for piece in range(0, chunk, TILE):
-                offset = lax.rem(at - start - piece + days, days)
+            for step in steps:
+                offset = lax.rem(at - step * chunk + days, days)
                 folded = lax.rem(offset, days // 2)
                 sums.append(toeplitz_sum[:, pl.ds(pl.multiple_of(folded, TILE), TILE)])
                 diffs.append(toeplitz_diff[:, pl.ds(pl.multiple_of(offset, TILE), TILE)])
@@ -372,10 +375,8 @@
             sum_part = acc[:, low_at] + dot(total, jnp.concatenate(sums, axis=0))
             diff_part = acc[:, high_at] + dot(difference, jnp.concatenate(diffs, axis=0))
             if last:
-                staged[:, low_at] = (sum_part + diff_part).astype(jnp.bfloat16)
-                staged[:, high_at] = (sum_part - diff_part).astype(jnp.bfloat16)
-                pltpu.make_async_copy(staged.at[:, low_at], out.at[:, low_at], out_sem.at[2 * index]).start()
-                pltpu.make_async_copy(staged.at[:, high_at], out.at[:, high_at], out_sem.at[2 * index + 1]).start()
+                out[:, low_at] = (sum_part + diff_part).astype(jnp.bfloat16)
+                out[:, high_at] = (sum_part - diff_part).astype(jnp.bfloat16)
             else:
                 acc[:, low_at] = sum_part
                 acc[:, high_at] = diff_part
@@ -396,14 +397,17 @@
         def _():
             mix_stage(turn - LEAD)
 
-        @pl.when(turn >= LEAD + 1)
-        def _():
-            filter_stage(turn - LEAD - 1, False)
+        mixed = turn - LEAD
+
+        @pl.when((mixed >= 2) & (lax.rem(mixed + chunks, 2) == 0))
+        def _():
+            filter_stage((mixed - 2, mixed - 1), False)
 
         return carry
 
     lax.fori_loop(0, chunks + LEAD, body, 0)
-    filter_stage(chunks - 1, True)
+    filter_stage((chunks - 2,), False)
+    filter_stage((chunks - 1,), True)
 
     def drain(step, carry):
         cross(step).wait_send()
@@ -431,11 +435,6 @@
     @pl.when(low & takes_up)
     def _():
         tiles_down().wait_send()
-
-    for index in range(days // TILE):
-        half_tiles = days // 2 // TILE
-        at = pl.ds((index // 2 + index % 2 * half_tiles) * TILE, TILE)
-        pltpu.make_async_copy(staged.at[:, at], out.at[:, at], out_sem.at[index]).wait()
 
 
 def fused(factor_rows, noise, time_kernel, region_of_block):
@@ -449,13 +448,12 @@
     pair = [pltpu.SemaphoreType.DMA((chunks,))] * 2
     return pl.pallas_call(
         sample_kernel,
-        out_shape=jax.ShapeDtypeStruct((rows, days), half),
+        out_shape=pltpu.VMEM((rows, days), half),
         in_specs=[hbm, hbm, vmem, pl.BlockSpec(memory_space=pltpu.SMEM)],
-        out_specs=hbm,
+        out_specs=vmem,
         scratch_shapes=[
             pltpu.VMEM((width, 4 * width), half),
             pltpu.VMEM((width, local_days), half),
-            pltpu.VMEM((rows, days), half),
             pltpu.VMEM((width, 4 * width), half),
             pltpu.VMEM((width, 2 * width), half),
             pltpu.VMEM((width, 2 * width), half),
@@ -470,10 +468,9 @@
             pltpu.VMEM((rows, days), jnp.float32),
         ]
         + pair * 4
-        + [pltpu.SemaphoreType.DMA((days // TILE,))]
         + [pltpu.SemaphoreType.DMA] * 4,
         compiler_params=pltpu.CompilerParams(
-            collective_id=0, has_side_effects=True, vmem_limit_bytes=60 * 1024 * 1024
+            collective_id=0, has_side_effects=True, vmem_limit_bytes=48 * 1024 * 1024
         ),
         cost_estimate=pl.CostEstimate(
             flops=rows * days * days + 8 * width * width * local_days,
@@ -490,8 +487,8 @@
 
     def program(factor_rows, noise, time_kernel, region_of_block):
         width, local_days = noise.shape
-        fits = width == 2 * TILE and factor_rows.shape[1] == 4 * width
-        fits = fits and 2 * local_days == time_kernel.shape[0] and local_days % CHUNK == 0 and local_days >= AHEAD * CHUNK
+        fits = width == 2 * TILE and CHUNK == TILE and factor_rows.shape[1] == 4 * width
+        fits = fits and 2 * local_days == time_kernel.shape[0] and local_days % (2 * CHUNK) == 0 and local_days >= AHEAD * CHUNK
         run = fused if paired and fits else on_device
         return run(factor_rows, noise, time_kernel, region_of_block)
 

time: 115 us -> 116 us (level)
  Pallas kernels: 110 us -> 112 us
  local copies, waits for them, and re-layouts: 4.64 us -> 3.43 us
    pallas_call x1, Pallas kernels: 110 us -> 112 us  [fused(): pl.pallas_call(sample_kernel, out_shape=pltpu.VMEM((rows, days), half), i...]
    unnamed x1 -> x5, local copies, waits for them, and re-layouts: 4.64 us -> 3.43 us
where the time goes in v4:
time: 116 us
  Pallas kernels  112 us (97%)
  local copies, waits for them, and re-layouts  3.43 us (3%)
    pallas_call x1, Pallas kernels, fused(): pl.pallas_call(sample_kernel, out_shape=pltpu.VMEM((rows, days), half), i...  112 us
    unnamed x5, local copies, waits for them, and re-layouts  3.43 us

profile of v4, /device:TPU:9, one launch (start us, length us, event | category | flops | bytes accessed | tf_op | source)
XLA Modules:
  0.0 115.7 jit_solution(12837331018911590606)
XLA Ops:
  0.0 0.0 copy-start
  0.0 0.8 copy-done
  0.8 0.0 copy-start.1
  0.8 0.7 copy-done.1
  1.4 112.3 %shard_map.46 = bf16[256,8192]{1,0:T(8,128)(2,1)S(1)} custom-call(bf16[512,2048]{1,0:T(8,128)(2,1)} %factor_hbm.1, bf16[512,4096]{1,0:T(8,128)(2,1)} %noise_hbm.1, f32[1,8192]{1,0:T(1,128)S(1)} %bitcast.1, s32[8]{0:T(128)S(1)} %copy-done.1), custom_call_target="tpu_custom_call" | custom-call | flops 25769803776 | bytes 10485760 | tf_op jit(solution)/shard_map/pallas_call | solution.py:449
  113.7 2.0 %copy.6 = bf16[256,8192]{1,0:T(8,128)(2,1)} copy(bf16[256,8192]{1,0:T(8,128)(2,1)S(1)} %shard_map.46) | data formatting | bytes 8388608
Async XLA Ops:
  0.0 0.8 copy-start
  0.8 0.7 copy-start.1

commit v5 on v4

--- a/solution.py
+++ b/solution.py
@@ -10,7 +10,8 @@
 FIRST = 64
 CHUNK = 256
 TILE = 256
-AHEAD = 6
+AHEAD = 4
+PENDING = 2
 LAG = 2
 LEAD = 4
 MESH = pl.DeviceIdType.MESH
@@ -310,6 +311,10 @@
         def _():
             side(step).wait_recv()
 
+        @pl.when(low & sends_up & (step >= PENDING))
+        def _():
+            up_partial(step - PENDING).wait_send()
+
         @pl.when(low & sends_up)
         def _():
             for part in range(0, width, rows):
@@ -420,7 +425,7 @@
         def _():
             sib_copy(step).wait_send()
 
-        @pl.when(low & sends_up)
+        @pl.when(low & sends_up & (step + PENDING >= chunks))
         def _():
             up_partial(step).wait_send()
 
@@ -470,7 +475,7 @@
         + pair * 4
         + [pltpu.SemaphoreType.DMA] * 4,
         compiler_params=pltpu.CompilerParams(
-            collective_id=0, has_side_effects=True, vmem_limit_bytes=48 * 1024 * 1024
+            collective_id=0, has_side_effects=True, vmem_limit_bytes=56 * 1024 * 1024
         ),
         cost_estimate=pl.CostEstimate(
             flops=rows * days * days + 8 * width * width * local_days,

time: 116 us -> 115 us (level)
  local copies, waits for them, and re-layouts: 3.43 us -> 2.02 us
    unnamed x5 -> x1, local copies, waits for them, and re-layouts: 3.43 us -> 2.02 us
where the time goes in v5:
time: 115 us
  Pallas kernels  113 us (98%)
  local copies, waits for them, and re-layouts  2.02 us (2%)
    pallas_call x1, Pallas kernels, fused(): pl.pallas_call(sample_kernel, out_shape=pltpu.VMEM((rows, days), half), i...  113 us

profile of v5, /device:TPU:9, one launch (start us, length us, event | category | flops | bytes accessed | tf_op | source)
XLA Modules:
  0.0 114.6 jit_solution(9351458649340231776)
XLA Ops:
  0.0 112.6 %shard_map.46 = bf16[256,8192]{1,0:T(8,128)(2,1)S(1)} custom-call(bf16[512,2048]{1,0:T(8,128)(2,1)} %factor_hbm.1, bf16[512,4096]{1,0:T(8,128)(2,1)} %noise_hbm.1, f32[1,8192]{1,0:T(1,128)} %bitcast.1, s32[8]{0:T(128)} %regions.1), custom_call_target="tpu_custom_call" | custom-call | flops 25769803776 | bytes 10485760 | tf_op jit(solution)/shard_map/pallas_call | solution.py:454
  112.6 2.0 %copy.6 = bf16[256,8192]{1,0:T(8,128)(2,1)} copy(bf16[256,8192]{1,0:T(8,128)(2,1)S(1)} %shard_map.46) | data formatting | bytes 8388608

commit v6 on v5

--- a/solution.py
+++ b/solution.py
@@ -10,10 +10,11 @@
 FIRST = 64
 CHUNK = 256
 TILE = 256
-AHEAD = 4
-PENDING = 2
-LAG = 2
-LEAD = 4
+AHEAD = 6
+EXTRA = 2
+PENDING = 4
+LAG = 1
+LEAD = 3
 MESH = pl.DeviceIdType.MESH
 
 
@@ -120,7 +121,7 @@
     factor_hbm, noise_hbm, time_kernel, regions, out,
     factor, noise, weights, partial_weights, above, up_in, side_in, shared,
     kept, given, got, toeplitz_sum, toeplitz_diff, acc,
-    up_send, up_recv, side_send, side_recv, sib_send, sib_recv, x_send, x_recv, tile_send, tile_recv, factor_sem, noise_sem,
+    up_send, up_recv, side_send, side_recv, sib_send, sib_recv, x_send, x_recv, extra_send, tile_send, tile_recv, hop_send, hop_recv, far_send, far_recv, factor_sem, noise_sem,
 ):
     blocks = lax.axis_size("blk")
     block = lax.axis_index("blk")
@@ -158,8 +159,22 @@
     def cross(step):
         return remote(given.at[step], got.at[step], x_send.at[step], x_recv.at[step], {"tm": 1 - half})
 
-    def tiles_down():
-        return remote(factor_hbm.at[:, pl.ds(2 * width, 2 * width)], above, tile_send, tile_recv, {"blk": block - 2})
+    def extra(index):
+        step = chunks - EXTRA + index
+        return remote(shared.at[step], up_in.at[step], extra_send.at[index], up_recv.at[step], {"blk": block + 3})
+
+    near_slot, far_slot = pl.ds(0, width), pl.ds(width, width)
+
+    def tile_down():
+        source = factor_hbm.at[:, pl.ds(2 * width, width)]
+        return remote(source, above.at[:, near_slot], tile_send, tile_recv, {"blk": block - 2})
+
+    def tile_hop():
+        source = factor_hbm.at[:, pl.ds(3 * width, width)]
+        return remote(source, above.at[:, far_slot], hop_send, hop_recv, {"blk": sib})
+
+    def far_down():
+        return remote(above.at[:, far_slot], above.at[:, far_slot], far_send, far_recv, {"blk": block - 3})
 
     load_factor = pltpu.make_async_copy(factor_hbm, factor, factor_sem)
     load_noise = pltpu.make_async_copy(noise_hbm, noise, noise_sem)
@@ -176,20 +191,33 @@
     def _():
         pl.semaphore_signal(barrier, inc=1, device_id={"blk": block + 2}, device_id_type=MESH)
 
-    pl.semaphore_wait(barrier, 2 + jnp.where(first_chip, 0, 1) + jnp.where(last_chip, 0, 1))
-
     low = core == 0
     high = core == 1
     sends_up = jnp.logical_not(last_chip)
     takes_up = jnp.logical_not(first_chip)
 
+    @pl.when(low & sends_up)
+    def _():
+        pl.semaphore_signal(barrier, inc=1, device_id={"blk": block + 3}, device_id_type=MESH)
+
+    @pl.when(high & takes_up)
+    def _():
+        pl.semaphore_signal(barrier, inc=1, device_id={"blk": block - 3}, device_id_type=MESH)
+
+    diagonal = jnp.where((low & sends_up) | (high & takes_up), 1, 0)
+    pl.semaphore_wait(barrier, 2 + jnp.where(first_chip, 0, 1) + jnp.where(last_chip, 0, 1) + diagonal)
+
     @pl.when(low & takes_up)
     def _():
-        tiles_down().start()
+        tile_hop().start()
+        tile_down().start()
 
     @pl.when(high & sends_up)
     def _():
-        for step in range(AHEAD):
+        up_noise(0).start()
+        for index in range(EXTRA):
+            sib_copy(chunks - EXTRA + index).start()
+        for step in range(1, AHEAD):
             up_noise(step).start()
 
     @pl.when(low)
@@ -198,6 +226,17 @@
             sib_copy(step).start()
 
     load_noise.start()
+
+    @pl.when(high & takes_up)
+    def _():
+        tile_hop().wait_recv()
+        far_down().start()
+
+    @pl.when(low & sends_up)
+    def _():
+        for index in range(EXTRA):
+            sib_copy(chunks - EXTRA + index).wait_recv()
+            extra(index).start()
 
     def valid(index, back):
         inside = index >= back
@@ -264,7 +303,8 @@
 
     @pl.when(low & sends_up)
     def _():
-        tiles_down().wait_recv()
+        tile_down().wait_recv()
+        far_down().wait_recv()
         uses = valid(jnp.minimum(block + 2, blocks - 1), 3)
 
         def make_partial_weights(index, carry):
@@ -287,7 +327,7 @@
     def send_stage(step):
         nothing = jnp.zeros((width, chunk), jnp.bfloat16)
 
-        @pl.when(high & sends_up & (step + AHEAD < chunks))
+        @pl.when(high & sends_up & (step + AHEAD < chunks - EXTRA))
         def _():
             up_noise(step).wait_send()
             up_noise(step + AHEAD).start()
@@ -310,6 +350,11 @@
         @pl.when(low & takes_up)
         def _():
             side(step).wait_recv()
+
+        for index in range(EXTRA):
+            @pl.when(low & sends_up & (step == chunks - EXTRA + index))
+            def _():
+                extra(index).wait_send()
 
         @pl.when(low & sends_up & (step >= PENDING))
         def _():
@@ -404,14 +449,13 @@
 
         mixed = turn - LEAD
 
-        @pl.when((mixed >= 2) & (lax.rem(mixed + chunks, 2) == 0))
-        def _():
-            filter_stage((mixed - 2, mixed - 1), False)
+        @pl.when(mixed >= 1)
+        def _():
+            filter_stage((mixed - 1,), False)
 
         return carry
 
     lax.fori_loop(0, chunks + LEAD, body, 0)
-    filter_stage((chunks - 2,), False)
     filter_stage((chunks - 1,), True)
 
     def drain(step, carry):
@@ -429,7 +473,7 @@
         def _():
             up_partial(step).wait_send()
 
-        @pl.when(high & sends_up & (step + AHEAD >= chunks))
+        @pl.when(high & sends_up & (step + AHEAD >= chunks - EXTRA) & (step < chunks - EXTRA))
         def _():
             up_noise(step).wait_send()
 
@@ -437,9 +481,19 @@
 
     lax.fori_loop(0, chunks, drain, 0)
 
+    @pl.when(high & sends_up)
+    def _():
+        for index in range(EXTRA):
+            sib_copy(chunks - EXTRA + index).wait_send()
+
     @pl.when(low & takes_up)
     def _():
-        tiles_down().wait_send()
+        tile_hop().wait_send()
+        tile_down().wait_send()
+
+    @pl.when(high & takes_up)
+    def _():
+        far_down().wait_send()
 
 
 def fused(factor_rows, noise, time_kernel, region_of_block):
@@ -473,7 +527,8 @@
             pltpu.VMEM((rows, days), jnp.float32),
         ]
         + pair * 4
-        + [pltpu.SemaphoreType.DMA] * 4,
+        + [pltpu.SemaphoreType.DMA((EXTRA,))]
+        + [pltpu.SemaphoreType.DMA] * 8,
         compiler_params=pltpu.CompilerParams(
             collective_id=0, has_side_effects=True, vmem_limit_bytes=56 * 1024 * 1024
         ),
@@ -493,7 +548,7 @@
     def program(factor_rows, noise, time_kernel, region_of_block):
         width, local_days = noise.shape
         fits = width == 2 * TILE and CHUNK == TILE and factor_rows.shape[1] == 4 * width
-        fits = fits and 2 * local_days == time_kernel.shape[0] and local_days % (2 * CHUNK) == 0 and local_days >= AHEAD * CHUNK
+        fits = fits and 2 * local_days == time_kernel.shape[0] and local_days % CHUNK == 0 and local_days >= (AHEAD + EXTRA) * CHUNK
         run = fused if paired and fits else on_device
         return run(factor_rows, noise, time_kernel, region_of_block)
 

time: 115 us -> 112 us (0.974)
  Pallas kernels: 113 us -> 109 us
    pallas_call x1, Pallas kernels: 113 us -> 109 us  [fused(): pl.pallas_call(sample_kernel, out_shape=pltpu.VMEM((rows, days), half), i...]
where the time goes in v6:
time: 112 us; the launch traced here: 111 us
  Pallas kernels  109 us (97%)
  local copies, waits for them, and re-layouts  2.02 us (2%)
    pallas_call x1, Pallas kernels, fused(): pl.pallas_call(sample_kernel, out_shape=pltpu.VMEM((rows, days), half), i...  109 us

profile of v6, /device:TPU:9, one launch (start us, length us, event | category | flops | bytes accessed | tf_op | source)
XLA Modules:
  0.0 111.4 jit_solution(4978151441735320004)
XLA Ops:
  0.0 109.4 %shard_map.46 = bf16[256,8192]{1,0:T(8,128)(2,1)S(1)} custom-call(bf16[512,2048]{1,0:T(8,128)(2,1)} %factor_hbm.1, bf16[512,4096]{1,0:T(8,128)(2,1)} %noise_hbm.1, f32[1,8192]{1,0:T(1,128)} %bitcast.1, s32[8]{0:T(128)} %regions.1), custom_call_target="tpu_custom_call" | custom-call | flops 25769803776 | bytes 10485760 | tf_op jit(solution)/shard_map/pallas_call | solution.py:508
  109.4 2.0 %copy.6 = bf16[256,8192]{1,0:T(8,128)(2,1)} copy(bf16[256,8192]{1,0:T(8,128)(2,1)S(1)} %shard_map.46) | data formatting | bytes 8388608

commit v7 on v6

--- a/solution.py
+++ b/solution.py
@@ -290,16 +290,16 @@
 
         lax.fori_loop(0, TILE // 16, add_strip, 0)
 
-    early, late = time_kernel[:, pl.ds(0, days // 2)], time_kernel[:, pl.ds(days // 2, days // 2)]
-    make_toeplitz(0.5 * (early + late), toeplitz_sum)
-    difference = 0.5 * (early - late)
-    make_toeplitz(jnp.concatenate([difference, -difference], axis=1), toeplitz_diff)
-
     def clear(index, carry):
         acc[:, pl.ds(pl.multiple_of(index * TILE, TILE), TILE)] = jnp.zeros((rows, TILE), jnp.float32)
         return carry
 
-    lax.fori_loop(0, days // TILE, clear, 0)
+    def make_tables():
+        early, late = time_kernel[:, pl.ds(0, days // 2)], time_kernel[:, pl.ds(days // 2, days // 2)]
+        make_toeplitz(0.5 * (early + late), toeplitz_sum)
+        difference = 0.5 * (early - late)
+        make_toeplitz(jnp.concatenate([difference, -difference], axis=1), toeplitz_diff)
+        lax.fori_loop(0, days // TILE, clear, 0)
 
     @pl.when(low & sends_up)
     def _():
@@ -432,7 +432,7 @@
                 acc[:, high_at] = diff_part
             return carry
 
-        lax.fori_loop(0, days // 2 // TILE, one, 0, unroll=4)
+        lax.fori_loop(0, days // 2 // TILE, one, 0, unroll=16)
 
     def body(turn, carry):
         @pl.when(turn < chunks)
@@ -442,6 +442,10 @@
         @pl.when((turn >= LAG) & (turn < chunks + LAG))
         def _():
             partial_stage(turn - LAG)
+
+        @pl.when(turn == LEAD - 1)
+        def _():
+            make_tables()
 
         @pl.when((turn >= LEAD) & (turn < chunks + LEAD))
         def _():

time: 112 us -> 108 us (0.964)
  Pallas kernels: 109 us -> 105 us
    pallas_call x1, Pallas kernels: 109 us -> 105 us  [fused(): pl.pallas_call(sample_kernel, out_shape=pltpu.VMEM((rows, days), half), i...]
where the time goes in v7:
time: 108 us; the launch traced here: 107 us
  Pallas kernels  105 us (97%)
  local copies, waits for them, and re-layouts  2.02 us (2%)
    pallas_call x1, Pallas kernels, fused(): pl.pallas_call(sample_kernel, out_shape=pltpu.VMEM((rows, days), half), i...  105 us

profile of v7, /device:TPU:9, one launch (start us, length us, event | category | flops | bytes accessed | tf_op | source)
XLA Modules:
  0.0 107.4 jit_solution(11485446667972736591)
XLA Ops:
  0.0 105.4 %shard_map.46 = bf16[256,8192]{1,0:T(8,128)(2,1)S(1)} custom-call(bf16[512,2048]{1,0:T(8,128)(2,1)} %factor_hbm.1, bf16[512,4096]{1,0:T(8,128)(2,1)} %noise_hbm.1, f32[1,8192]{1,0:T(1,128)} %bitcast.1, s32[8]{0:T(128)} %regions.1), custom_call_target="tpu_custom_call" | custom-call | flops 25769803776 | bytes 10485760 | tf_op jit(solution)/shard_map/pallas_call | solution.py:512
  105.4 2.0 %copy.6 = bf16[256,8192]{1,0:T(8,128)(2,1)} copy(bf16[256,8192]{1,0:T(8,128)(2,1)S(1)} %shard_map.46) | data formatting | bytes 8388608

commit v8 on v7

--- a/solution.py
+++ b/solution.py
@@ -11,8 +11,8 @@
 CHUNK = 256
 TILE = 256
 AHEAD = 6
-EXTRA = 2
-PENDING = 4
+EXTRA = 1
+PENDING = 8
 LAG = 1
 LEAD = 3
 MESH = pl.DeviceIdType.MESH

time: 108 us -> 108 us (level)
  no operation moved by 1% of the time
where the time goes in v8:
time: 108 us; the launch traced here: 107 us
  Pallas kernels  105 us (97%)
  local copies, waits for them, and re-layouts  2.02 us (2%)
    pallas_call x1, Pallas kernels, fused(): pl.pallas_call(sample_kernel, out_shape=pltpu.VMEM((rows, days), half), i...  105 us

profile of v8, /device:TPU:9, one launch (start us, length us, event | category | flops | bytes accessed | tf_op | source)
XLA Modules:
  0.0 107.4 jit_solution(411258775564116802)
XLA Ops:
  0.0 105.4 %shard_map.46 = bf16[256,8192]{1,0:T(8,128)(2,1)S(1)} custom-call(bf16[512,2048]{1,0:T(8,128)(2,1)} %factor_hbm.1, bf16[512,4096]{1,0:T(8,128)(2,1)} %noise_hbm.1, f32[1,8192]{1,0:T(1,128)} %bitcast.1, s32[8]{0:T(128)} %regions.1), custom_call_target="tpu_custom_call" | custom-call | flops 25769803776 | bytes 10485760 | tf_op jit(solution)/shard_map/pallas_call | solution.py:512
  105.4 2.0 %copy.6 = bf16[256,8192]{1,0:T(8,128)(2,1)} copy(bf16[256,8192]{1,0:T(8,128)(2,1)S(1)} %shard_map.46) | data formatting | bytes 8388608
